TPU v7x, 1024 devices: a whole 4x4x32 slice. The times are simulated.
1024 devices in a mesh: dp: 16 (over x, y), expert: 64 (over z, core).
Axes of the slice: x: 4, y: 4, z: 32, core: 2. Of those that a mesh axis runs over, the one named last changes fastest.
Arguments:
- tokens: bfloat16 [131072, 2048], P(('dp', 'expert')), may hold values from -6 to 6
- routes: int32 [131072, 1], P(('dp', 'expert')), may hold values from 0 to 63; in each aligned block of 128 rows (0 to 127, 128 to 255, ...) at most 3 rows name the same one
- gates: float32 [131072, 1], P(('dp', 'expert')), may hold values from 0.2 to 1
- w_in: bfloat16 [64, 2048, 768], P('expert'), may hold values from -0.125 to 0.125
- w_out: bfloat16 [64, 768, 2048], P('expert'), may hold values from -0.21875 to 0.21875
- out_grad: bfloat16 [131072, 2048], P(('dp', 'expert')), may hold values from -3 to 3
Outputs:
- mixed: bfloat16 [131072, 2048], P(('dp', 'expert'))
- grad_tokens: bfloat16 [131072, 2048], P(('dp', 'expert'))
- grad_gates: float32 [131072, 1], P(('dp', 'expert'))
- grad_w_in: float32 [64, 2048, 768], P('expert', 'dp')
- grad_w_out: float32 [64, 768, 2048], P('expert', None, 'dp')
Inputs may be any that keep to these rules, and one draw needn't show every extreme that they name: `routes`: each row names one expert. Among the rows of one device no expert is named more than 3 times, a bound that some block reaches.
All inputs are finite; a program needn't handle non-finite values.
Results may differ from a plain program's by a relative error of at most 0.015.
Values may be sent and summed in bfloat16 or wider, within the bound.
A program may use at most 64 MiB of HBM per device.

v0:
```python
import jax
import jax.numpy as jnp
from jax import lax
from jax.sharding import PartitionSpec as P


def contract_rows(left, right):
    return lax.dot_general(
        left, right, (((0,), (0,)), ((), ())), preferred_element_type=jnp.float32
    )


def contract_last(left, right):
    return lax.dot_general(
        left, right, (((1,), (1,)), ((), ())), preferred_element_type=jnp.float32
    )


def local(tokens, routes, gates, w_in, w_out, out_grad):
    tok_rows, width = tokens.shape
    top = routes.shape[1]
    experts = lax.axis_size("expert")
    capacity = max(2, 3 * tok_rows * top // (2 * experts))
    pairs = tok_rows * top
    slots_all = experts * capacity
    flat = routes.reshape(pairs)
    onehot = (flat[:, None] == jnp.arange(experts, dtype=jnp.int32)[None, :]).astype(jnp.int32)
    earlier = jnp.cumsum(onehot, axis=0) - onehot
    slot = jnp.sum(onehot * earlier, axis=1)
    place = flat * capacity + slot
    select = jnp.arange(slots_all, dtype=jnp.int32)[:, None] == place[None, :]
    select_bf = select.astype(jnp.bfloat16)
    spread = jnp.any(select.reshape(slots_all, tok_rows, top), axis=2).astype(jnp.bfloat16)
    send_tok = jnp.dot(spread, tokens, preferred_element_type=jnp.float32).astype(jnp.bfloat16)
    scaled = (gates[:, :, None] * out_grad.astype(jnp.float32)[:, None, :]).astype(jnp.bfloat16)
    send_grad = jnp.dot(
        select_bf, scaled.reshape(pairs, width), preferred_element_type=jnp.float32
    ).astype(jnp.bfloat16)
    recv_tok, recv_grad = (
        lax.all_to_all(
            send_tok.reshape(experts, capacity, width),
            "expert",
            split_axis=0,
            concat_axis=0,
            tiled=True,
        ),
        lax.all_to_all(
            send_grad.reshape(experts, capacity, width),
            "expert",
            split_axis=0,
            concat_axis=0,
            tiled=True,
        ),
    )
    slots_x = recv_tok.reshape(slots_all, width)
    slots_g = recv_grad.reshape(slots_all, width)
    w_first = w_in[0]
    w_second = w_out[0]
    pre = jnp.dot(slots_x, w_first, preferred_element_type=jnp.float32)
    hidden = jax.nn.silu(pre).astype(jnp.bfloat16)
    expert_out = jnp.dot(hidden, w_second, preferred_element_type=jnp.float32).astype(jnp.bfloat16)
    sig = jax.nn.sigmoid(pre)
    grad_hidden = contract_last(slots_g, w_second)
    grad_pre = (grad_hidden * sig * (1.0 + pre * (1.0 - sig))).astype(jnp.bfloat16)
    grad_slots = contract_last(grad_pre, w_first).astype(jnp.bfloat16)
    back_out, back_grad = (
        lax.all_to_all(
            expert_out.reshape(experts, capacity, width),
            "expert",
            split_axis=0,
            concat_axis=0,
            tiled=True,
        ),
        lax.all_to_all(
            grad_slots.reshape(experts, capacity, width),
            "expert",
            split_axis=0,
            concat_axis=0,
            tiled=True,
        ),
    )
    picked = contract_rows(select_bf, back_out.reshape(slots_all, width)).reshape(
        tok_rows, top, width
    )
    mixed = jnp.sum(gates[:, :, None] * picked, axis=1).astype(jnp.bfloat16)
    grad_gates = jnp.sum(picked * out_grad.astype(jnp.float32)[:, None, :], axis=2)
    grad_tokens = contract_rows(spread, back_grad.reshape(slots_all, width)).astype(jnp.bfloat16)
    cols = slots_x
    grad_first = lax.psum_scatter(
        contract_rows(cols, grad_pre).astype(jnp.bfloat16), "dp", scatter_dimension=0, tiled=True
    ).astype(jnp.float32)
    cols = slots_g
    grad_second = (
        lax.psum_scatter(
            contract_rows(cols, hidden).astype(jnp.bfloat16), "dp", scatter_dimension=0, tiled=True
        )
        .astype(jnp.float32)
        .T
    )
    return (mixed, grad_tokens, grad_gates, grad_first[None], grad_second[None])


def solution(mesh):
    placed = (
        P(("dp", "expert"), None),
        P(("dp", "expert"), None),
        P(("dp", "expert"), None),
        P("expert", None, None),
        P("expert", None, None),
        P(("dp", "expert"), None),
    )
    return jax.shard_map(
        local,
        mesh=mesh,
        in_specs=placed,
        out_specs=(
            P(("dp", "expert"), None),
            P(("dp", "expert"), None),
            P(("dp", "expert"), None),
            P("expert", "dp", None),
            P("expert", None, "dp"),
        ),
        check_vma=False,
    )
```

profile of v0, /device:TPU:1, one launch (start us, length us, event | category | flops | bytes accessed | tf_op | source)
XLA Modules:
  0.0 533.2 jit_solution(16399997028280441106)
XLA Ops:
  9.8 2.3 convolution_convert_fusion.3
  12.1 3.3 reshape.105
  15.3 30.6 %all-to-all-start = ((bf16[64,3,2048]{2,1,0:T(4,128)(2,1)}), bf16[64,3,2048]{2,1,0:T(4,128)(2,1)}, u32[]{:S(2)}, u32[]{:S(2)}) async-start(bf16[64,3,2048]{2,1,0:T(4,128)(2,1)} %reshape.105), calls=%async_computation | async-start | bytes 2097152 | tf_op jit(solution)/shard_map/all_to_all | solution.py:40
  46.0 2.4 convolution_convert_fusion.2
  48.3 3.3 reshape.109
  51.6 102.4 %all-to-all-done = bf16[64,3,2048]{2,1,0:T(4,128)(2,1)} async-done(((bf16[64,3,2048]{2,1,0:T(4,128)(2,1)}), bf16[64,3,2048]{2,1,0:T(4,128)(2,1)}, u32[]{:S(2)}, u32[]{:S(2)}) %all-to-all-start) | async-done | bytes 786464 | tf_op jit(solution)/shard_map/all_to_all | solution.py:40
  154.0 7.9 %all-to-all-start.2 = ((bf16[64,3,2048]{2,1,0:T(4,128)(2,1)}), bf16[64,3,2048]{2,1,0:T(4,128)(2,1)}, u32[]{:S(2)}, u32[]{:S(2)}) async-start(bf16[64,3,2048]{2,1,0:T(4,128)(2,1)} %reshape.109), calls=%async_computation.2 | async-start | bytes 2097152 | tf_op jit(solution)/shard_map/all_to_all | solution.py:47
  161.9 3.2 reshape.106
  165.1 2.7 fusion.6
  167.8 102.1 %all-to-all-done.2 = bf16[64,3,2048]{2,1,0:T(4,128)(2,1)} async-done(((bf16[64,3,2048]{2,1,0:T(4,128)(2,1)}), bf16[64,3,2048]{2,1,0:T(4,128)(2,1)}, u32[]{:S(2)}, u32[]{:S(2)}) %all-to-all-start.2) | async-done | bytes 786464 | tf_op jit(solution)/shard_map/all_to_all | solution.py:47
  269.9 3.2 reshape.110
  273.1 3.5 fusion.20
  278.6 3.3 reshape.111
  281.9 8.1 %all-to-all-start.3 = ((bf16[64,3,2048]{2,1,0:T(4,128)(2,1)}), bf16[64,3,2048]{2,1,0:T(4,128)(2,1)}, u32[]{:S(2)}, u32[]{:S(2)}) async-start(bf16[64,3,2048]{2,1,0:T(4,128)(2,1)} %reshape.111), calls=%async_computation.3 | async-start | bytes 2097152 | tf_op jit(solution)/shard_map/all_to_all | solution.py:74
  290.0 4.0 convolution_convert_fusion
  294.1 3.8 fusion.11
  297.9 3.3 reshape.107
  301.2 96.8 %all-to-all-done.3 = bf16[64,3,2048]{2,1,0:T(4,128)(2,1)} async-done(((bf16[64,3,2048]{2,1,0:T(4,128)(2,1)}), bf16[64,3,2048]{2,1,0:T(4,128)(2,1)}, u32[]{:S(2)}, u32[]{:S(2)}) %all-to-all-start.3) | async-done | bytes 786464 | tf_op jit(solution)/shard_map/all_to_all | solution.py:74
  397.9 8.3 %all-to-all-start.1 = ((bf16[64,3,2048]{2,1,0:T(4,128)(2,1)}), bf16[64,3,2048]{2,1,0:T(4,128)(2,1)}, u32[]{:S(2)}, u32[]{:S(2)}) async-start(bf16[64,3,2048]{2,1,0:T(4,128)(2,1)} %reshape.107), calls=%async_computation.1 | async-start | bytes 2097152 | tf_op jit(solution)/shard_map/all_to_all | solution.py:67
  406.3 3.9 convolution_convert_fusion.1
  410.2 3.2 reshape.112
  413.4 100.8 %all-to-all-done.1 = bf16[64,3,2048]{2,1,0:T(4,128)(2,1)} async-done(((bf16[64,3,2048]{2,1,0:T(4,128)(2,1)}), bf16[64,3,2048]{2,1,0:T(4,128)(2,1)}, u32[]{:S(2)}, u32[]{:S(2)}) %all-to-all-start.1) | async-done | bytes 786464 | tf_op jit(solution)/shard_map/all_to_all | solution.py:67
  514.2 3.2 reshape.108
  519.7 3.1 fusion.24
  (19 shorter events, 10.6 us)
Async XLA Ops:
  7.2 157.9 %copy-start = (bf16[1,2048,768]{2,1,0:T(8,128)(2,1)S(1)}, bf16[1,2048,768]{2,1,0:T(8,128)(2,1)}, u32[]{:S(2)}) copy-start(bf16[1,2048,768]{2,1,0:T(8,128)(2,1)} %param.9) | copy-start | bytes 9437188
  7.2 38.8 %copy-start.1 = (f32[128,1]{0,1:T(1,128)S(1)}, f32[128,1]{0,1:T(1,128)}, u32[]{:S(2)}) copy-start(f32[128,1]{0,1:T(1,128)} %param.8) | copy-start | bytes 1540
  15.3 138.7 %all-to-all-start = ((bf16[64,3,2048]{2,1,0:T(4,128)(2,1)}), bf16[64,3,2048]{2,1,0:T(4,128)(2,1)}, u32[]{:S(2)}, u32[]{:S(2)}) async-start(bf16[64,3,2048]{2,1,0:T(4,128)(2,1)} %reshape.105), calls=%async_computation | async-start | bytes 2097152 | tf_op jit(solution)/shard_map/all_to_all | solution.py:40
  154.0 115.8 %all-to-all-start.2 = ((bf16[64,3,2048]{2,1,0:T(4,128)(2,1)}), bf16[64,3,2048]{2,1,0:T(4,128)(2,1)}, u32[]{:S(2)}, u32[]{:S(2)}) async-start(bf16[64,3,2048]{2,1,0:T(4,128)(2,1)} %reshape.109), calls=%async_computation.2 | async-start | bytes 2097152 | tf_op jit(solution)/shard_map/all_to_all | solution.py:47
  281.9 116.1 %all-to-all-start.3 = ((bf16[64,3,2048]{2,1,0:T(4,128)(2,1)}), bf16[64,3,2048]{2,1,0:T(4,128)(2,1)}, u32[]{:S(2)}, u32[]{:S(2)}) async-start(bf16[64,3,2048]{2,1,0:T(4,128)(2,1)} %reshape.111), calls=%async_computation.3 | async-start | bytes 2097152 | tf_op jit(solution)/shard_map/all_to_all | solution.py:74
  290.0 232.8 %reduce-scatter.5.cloned.1.call-start = ((), (), s32[]{:S(2)}) async-start(), calls=%async_computation.7 | async-start | bytes 3342336 | tf_op jit(solution)/shard_map/reduce_scatter | solution.py:94
  397.9 116.3 %all-to-all-start.1 = ((bf16[64,3,2048]{2,1,0:T(4,128)(2,1)}), bf16[64,3,2048]{2,1,0:T(4,128)(2,1)}, u32[]{:S(2)}, u32[]{:S(2)}) async-start(bf16[64,3,2048]{2,1,0:T(4,128)(2,1)} %reshape.107), calls=%async_computation.1 | async-start | bytes 2097152 | tf_op jit(solution)/shard_map/all_to_all | solution.py:67
  406.2 118.4 %reduce-scatter.3.cloned.1.call-start = ((), (), s32[]{:S(2)}) async-start(), calls=%async_computation.6 | async-start | bytes 3342336 | tf_op jit(solution)/shard_map/reduce_scatter | solution.py:89
Sparse Core Ops, SparseCore 0:
  296.2 110.6 reduce-scatter.4
  412.5 110.9 reduce-scatter.2
where the time goes:
time: 536 us; the launch traced here: 533 us
  waiting for transfers between devices  402 us (75%)
  starting transfers between devices  54.9 us (10%)
  matrix products  29.9 us (6%)
  local copies, waits for them, and re-layouts  26.8 us (5%)
  between operations  14.1 us (3%)
    all_to_all x1, waiting for transfers between devices, local(): lax.all_to_all(send_tok.reshape(experts, capacity, width), 'expert', spli...  102 us
    all_to_all x1, waiting for transfers between devices, local(): lax.all_to_all(send_grad.reshape(experts, capacity, width), 'expert', spl...  102 us
    all_to_all x1, waiting for transfers between devices, local(): lax.all_to_all(expert_out.reshape(experts, capacity, width), 'expert', sp...  101 us
    all_to_all x1, waiting for transfers between devices, local(): lax.all_to_all(grad_slots.reshape(experts, capacity, width), 'expert', sp...  96.8 us
    all_to_all x1, starting transfers between devices, local(): lax.all_to_all(send_tok.reshape(experts, capacity, width), 'expert', spli...  30.6 us
    dot_general x4, matrix products, contract_rows(): lax.dot_general(left, right, (((0,), (0,)), ((), ())), preferred_element_...  13.2 us
  transfers between devices with their start and end apart: 6, of which 4 were waited for; matrix products, arithmetic and copies ran while one was open for 8% of the time, Pallas kernels for 0%

commit v1 on v0

v1 whole, which is shorter than its diff:
```python
import functools

import jax
import jax.numpy as jnp
from jax import lax
from jax.experimental import pallas as pl
from jax.experimental.pallas import tpu as pltpu
from jax.sharding import PartitionSpec as P

MESH = pl.DeviceIdType.MESH
LANES = 128
F32 = jnp.float32
BF16 = jnp.bfloat16


def dot(left, right, dims):
    return lax.dot_general(left, right, ((dims[0], dims[1]), ((), ())), preferred_element_type=F32)


def kernel(
    groups,
    experts,
    capacity,
    tok_hbm,
    grad_hbm,
    w_in_hbm,
    w_out_hbm,
    routes_ref,
    gates_ref,
    mixed_ref,
    grad_tok_ref,
    grad_gates_ref,
    first_ref,
    second_ref,
    tok,
    cot,
    w_in,
    w_out,
    select,
    stage,
    x_send,
    x_recv,
    g_send,
    g_recv,
    o_send,
    o_recv,
    b_send,
    b_recv,
    xs,
    gs,
    pre,
    hidden,
    grad_pre,
    first_send,
    first_recv,
    second_send,
    second_recv,
    load_sem,
    own_sem,
    send_sem,
    recv_sem,
):
    dp = lax.axis_index("dp")
    me = lax.axis_index("expert")
    z, core = me // 2, me % 2
    ring = experts // 2
    rows, width = tok.shape
    slots = experts * capacity
    chunks = width // LANES
    block = capacity * chunks
    hid = hidden.shape[1]

    loads = [
        pltpu.make_async_copy(source, target, load_sem.at[i])
        for i, (source, target) in enumerate(
            ((tok_hbm, tok), (grad_hbm, cot), (w_in_hbm, w_in), (w_out_hbm, w_out))
        )
    ]
    for load in loads:
        load.start()

    barrier = pltpu.get_barrier_semaphore()

    def greet_expert(k, _):
        pl.semaphore_signal(
            barrier, inc=1, device_id=(dp, (me + k) % experts), device_id_type=MESH
        )
        return 0

    def greet_group(k, _):
        pl.semaphore_signal(
            barrier, inc=1, device_id=((dp + k) % groups, me), device_id_type=MESH
        )
        return 0

    lax.fori_loop(1, experts, greet_expert, 0)
    lax.fori_loop(1, groups, greet_group, 0)

    def scatter(source, target, which):
        pltpu.make_async_copy(source.at[me], target.at[me], own_sem.at[which]).start()

        def send(place):
            pltpu.make_async_remote_copy(
                src_ref=source.at[place],
                dst_ref=target.at[me],
                send_sem=send_sem.at[which],
                recv_sem=recv_sem.at[which],
                device_id=(dp, place),
                device_id_type=MESH,
            ).start()

        def step(i, _):
            far = ring // 2 - (i + 1) // 2
            sign = 1 - 2 * (i % 2)
            there = (z + sign * far + ring) % ring
            send(there * 2 + core)
            send(there * 2 + 1 - core)
            return 0

        lax.fori_loop(0, ring - 1, step, 0)
        send(z * 2 + 1 - core)

    def arrived(target, which):
        others = target.at[pl.ds(0, target.shape[0] - 1)]
        pltpu.make_async_copy(target.at[0], target.at[0], own_sem.at[which]).wait()
        pltpu.make_async_copy(others, others, recv_sem.at[which]).wait()

    def sent(target, which):
        others = target.at[pl.ds(0, target.shape[0] - 1)]
        pltpu.make_async_copy(others, others, send_sem.at[which]).wait()

    def spread(j, value):
        stage[pl.ds(j, slots, stride=chunks), :] = value

    def gathered(j):
        return stage[pl.ds(j, slots, stride=chunks), :]

    def lanes(j):
        return pl.ds(pl.multiple_of(j * LANES, LANES), LANES)

    def to_blocks(target):
        def step(e, _):
            part = stage[pl.ds(pl.multiple_of(e * block, block), block), :]
            target[e] = part.astype(BF16)
            return 0

        lax.fori_loop(0, experts, step, 0, unroll=4)

    def from_blocks(source):
        def step(e, _):
            stage[pl.ds(pl.multiple_of(e * block, block), block), :] = source[e].astype(F32)
            return 0

        lax.fori_loop(0, experts, step, 0, unroll=4)

    def to_rows(source, target):
        from_blocks(source)

        def step(j, _):
            target[:, lanes(j)] = gathered(j).astype(BF16)
            return 0

        lax.fori_loop(0, chunks, step, 0)

    route = routes_ref[...]
    onehot = (route == lax.broadcasted_iota(jnp.int32, (rows, experts), 1)).astype(F32)
    before = (
        lax.broadcasted_iota(jnp.int32, (rows, rows), 0)
        > lax.broadcasted_iota(jnp.int32, (rows, rows), 1)
    ).astype(BF16)
    earlier = dot(before, onehot.astype(BF16), ((1,), (0,)))
    slot = jnp.sum(onehot * earlier, axis=1, keepdims=True).astype(jnp.int32)
    place = route * capacity + slot
    select[...] = (place == lax.broadcasted_iota(jnp.int32, (rows, slots), 1)).astype(BF16)

    loads[0].wait()

    def pick_tokens(j, _):
        spread(j, dot(select[...], tok[:, lanes(j)], ((0,), (0,))))
        return 0

    lax.fori_loop(0, chunks, pick_tokens, 0)
    to_blocks(x_send)
    pl.semaphore_wait(barrier, experts - 1 + groups - 1)
    scatter(x_send, x_recv, 0)

    loads[1].wait()

    def pick_grads(j, _):
        scaled = (gates_ref[...] * cot[:, lanes(j)].astype(F32)).astype(BF16)
        spread(j, dot(select[...], scaled, ((0,), (0,))))
        return 0

    lax.fori_loop(0, chunks, pick_grads, 0)
    to_blocks(g_send)
    scatter(g_send, g_recv, 1)

    loads[2].wait()
    loads[3].wait()
    arrived(x_recv, 0)
    to_rows(x_recv, xs)

    def wide(j):
        return pl.ds(pl.multiple_of(j * 256, 256), 256)

    def forward(j, _):
        value = dot(xs[...], w_in[:, wide(j)], ((1,), (0,)))
        pre[:, wide(j)] = value
        hidden[:, wide(j)] = (value / (1.0 + jnp.exp(-value))).astype(BF16)
        return 0

    lax.fori_loop(0, hid // 256, forward, 0)

    def project(j, _):
        value = dot(hidden[...], w_out[:, wide(j)], ((1,), (0,)))
        spread(2 * j, value[:, :LANES])
        spread(2 * j + 1, value[:, LANES:])
        return 0

    lax.fori_loop(0, width // 256, project, 0)
    to_blocks(o_send)
    scatter(o_send, o_recv, 2)

    arrived(g_recv, 1)
    to_rows(g_recv, gs)

    def backward(j, _):
        value = dot(gs[...], w_out[wide(j), :], ((1,), (1,)))
        at = pre[:, wide(j)]
        sig = 1.0 / (1.0 + jnp.exp(-at))
        grad_pre[:, wide(j)] = (value * sig * (1.0 + at * (1.0 - sig))).astype(BF16)
        return 0

    lax.fori_loop(0, hid // 256, backward, 0)

    def unproject(j, _):
        value = dot(grad_pre[...], w_in[wide(j), :], ((1,), (1,)))
        spread(2 * j, value[:, :LANES])
        spread(2 * j + 1, value[:, LANES:])
        return 0

    lax.fori_loop(0, width // 256, unproject, 0)
    to_blocks(b_send)
    scatter(b_send, b_recv, 3)

    def weight_terms(k, _):
        to = (dp + k) % groups
        first_send[to] = dot(xs[:, lanes(to)], grad_pre[...], ((0,), (0,))).astype(BF16)
        second_send[to] = dot(hidden[...], gs[:, lanes(to)], ((0,), (0,))).astype(BF16)
        return to

    def share(k, _):
        to = weight_terms(k, 0)
        for which, source, target in ((4, first_send, first_recv), (5, second_send, second_recv)):
            pltpu.make_async_remote_copy(
                src_ref=source.at[to],
                dst_ref=target.at[dp],
                send_sem=send_sem.at[which],
                recv_sem=recv_sem.at[which],
                device_id=(to, me),
                device_id_type=MESH,
            ).start()
        return 0

    lax.fori_loop(1, groups, share, 0)
    weight_terms(0, 0)
    for which, source, target in ((4, first_send, first_recv), (5, second_send, second_recv)):
        pltpu.make_async_copy(source.at[dp], target.at[dp], own_sem.at[which]).start()

    arrived(o_recv, 2)
    from_blocks(o_recv)
    grad_gates_ref[...] = jnp.zeros_like(grad_gates_ref)

    def mix(j, _):
        picked = dot(select[...], gathered(j).astype(BF16), ((1,), (0,)))
        mixed_ref[:, lanes(j)] = (gates_ref[...] * picked).astype(BF16)
        grad_gates_ref[...] += jnp.sum(
            picked * cot[:, lanes(j)].astype(F32), axis=1, keepdims=True
        )
        return 0

    lax.fori_loop(0, chunks, mix, 0)

    arrived(first_recv, 4)
    arrived(second_recv, 5)

    def add_terms(target, source):
        def step(r, _):
            part = pl.ds(pl.multiple_of(r * 16, 16), 16)
            total = source[0, part, :].astype(F32)
            for i in range(1, groups):
                total = total + source[i, part, :].astype(F32)
            target[part, :] = total
            return 0

        lax.fori_loop(0, target.shape[0] // 16, step, 0)

    add_terms(first_ref, first_recv)
    add_terms(second_ref, second_recv)

    arrived(b_recv, 3)
    from_blocks(b_recv)

    def unmix(j, _):
        picked = dot(select[...], gathered(j).astype(BF16), ((1,), (0,)))
        grad_tok_ref[:, lanes(j)] = picked.astype(BF16)
        return 0

    lax.fori_loop(0, chunks, unmix, 0)
    sent(x_send, 0)
    sent(g_send, 1)
    sent(o_send, 2)
    sent(b_send, 3)
    sent(first_send, 4)
    sent(second_send, 5)


def local(tokens, routes, gates, w_in, w_out, out_grad):
    groups, experts = lax.axis_size("dp"), lax.axis_size("expert")
    rows, width = tokens.shape
    capacity = max(2, 3 * rows * routes.shape[1] // (2 * experts))
    slots = experts * capacity
    hid = w_in.shape[2]
    chunks = width // LANES
    blocks = pltpu.VMEM((experts, capacity * chunks, LANES), BF16)
    first = pltpu.VMEM((groups, width // groups, hid), BF16)
    second = pltpu.VMEM((groups, hid, width // groups), BF16)
    vmem = pl.BlockSpec(memory_space=pltpu.VMEM)
    hbm = pl.BlockSpec(memory_space=pl.ANY)
    mixed, grad_tokens, grad_gates, grad_first, grad_second = pl.pallas_call(
        functools.partial(kernel, groups, experts, capacity),
        out_shape=(
            jax.ShapeDtypeStruct((rows, width), BF16),
            jax.ShapeDtypeStruct((rows, width), BF16),
            jax.ShapeDtypeStruct((rows, 1), F32),
            jax.ShapeDtypeStruct((width // groups, hid), F32),
            jax.ShapeDtypeStruct((hid, width // groups), F32),
        ),
        in_specs=[hbm, hbm, hbm, hbm, vmem, vmem],
        out_specs=[vmem] * 5,
        scratch_shapes=[
            pltpu.VMEM((rows, width), BF16),
            pltpu.VMEM((rows, width), BF16),
            pltpu.VMEM((width, hid), BF16),
            pltpu.VMEM((hid, width), BF16),
            pltpu.VMEM((rows, slots), BF16),
            pltpu.VMEM((slots * chunks, LANES), F32),
            *([blocks] * 8),
            pltpu.VMEM((slots, width), BF16),
            pltpu.VMEM((slots, width), BF16),
            pltpu.VMEM((slots, hid), F32),
            pltpu.VMEM((slots, hid), BF16),
            pltpu.VMEM((slots, hid), BF16),
            first,
            first,
            second,
            second,
            pltpu.SemaphoreType.DMA((4,)),
            pltpu.SemaphoreType.DMA((6,)),
            pltpu.SemaphoreType.DMA((6,)),
            pltpu.SemaphoreType.DMA((6,)),
        ],
        compiler_params=pltpu.CompilerParams(
            collective_id=0, has_side_effects=True, vmem_limit_bytes=50 * 2**20
        ),
        cost_estimate=pl.CostEstimate(
            flops=12 * slots * width * hid,
            bytes_accessed=12 * width * hid,
            transcendentals=2 * slots * hid,
        ),
    )(tokens, out_grad, w_in[0], w_out[0], routes, gates)
    return (mixed, grad_tokens, grad_gates, grad_first[None], grad_second[None])


def solution(mesh):
    placed = (
        P(("dp", "expert"), None),
        P(("dp", "expert"), None),
        P(("dp", "expert"), None),
        P("expert", None, None),
        P("expert", None, None),
        P(("dp", "expert"), None),
    )
    return jax.shard_map(
        local,
        mesh=mesh,
        in_specs=placed,
        out_specs=(
            P(("dp", "expert"), None),
            P(("dp", "expert"), None),
            P(("dp", "expert"), None),
            P("expert", "dp", None),
            P("expert", None, "dp"),
        ),
        check_vma=False,
    )
```

time: 536 us -> 349 us (0.65)
  the two profiles are of different devices: /device:TPU:1 before, /device:TPU:605 now
where the time goes in v1:
time: 349 us
  Pallas kernels  341 us (98%)
  local copies, waits for them, and re-layouts  7.26 us (2%)
    pallas_call x1, Pallas kernels, local(): pl.pallas_call(functools.partial(kernel, groups, experts, capacity), out_...  341 us
    unnamed x11, local copies, waits for them, and re-layouts  7.26 us

profile of v1, /device:TPU:605, one launch (start us, length us, event | category | flops | bytes accessed | tf_op | source)
XLA Modules:
  0.0 349.0 jit_solution(12965513871406221441)
XLA Ops:
  0.6 0.8 copy.11.routes_ref
  1.4 0.8 copy.12.gates_ref
  2.2 0.0 copy-start
  2.2 1.0 copy-done
  3.2 0.0 copy-start.1
  3.2 1.0 copy-done.1
  4.2 341.1 %shard_map.101 = (bf16[128,2048]{1,0:T(8,128)(2,1)S(1)}, bf16[128,2048]{1,0:T(8,128)(2,1)S(1)}, f32[128,1]{1,0:T(8,128)S(1)}, f32[128,768]{1,0:T(8,128)S(1)}, f32[768,128]{1,0:T(8,128)S(1)}) custom-call(bf16[128,2048]{1,0:T(8,128)(2,1)S(1)} %copy-done, bf16[128,2048]{1,0:T(8,128)(2,1)S(1)} %copy-done.1, bf16[2048,768]{1,0:T(8,128)(2,1)} %bitcast.6, ...), custom_call_target="tpu_custom_call" | custom-call | flops 3623878656 | bytes 18874368 | tf_op jit(solution)/shard_map/pallas_call | solution.py:330
  345.4 0.6 copy.13
  346.0 0.8 copy.18
  346.8 0.8 copy.19
  347.6 0.7 copy.20
  348.3 0.7 copy.21
Async XLA Ops:
  2.2 1.0 copy-start
  3.2 1.0 copy-start.1

commit v2 on v1

--- a/solution.py
+++ b/solution.py
@@ -1,4 +1,5 @@
 import functools
+import math
 
 import jax
 import jax.numpy as jnp
@@ -219,6 +220,7 @@
 
     lax.fori_loop(0, width // 256, project, 0)
     to_blocks(o_send)
+    sent(g_send, 1)
     scatter(o_send, o_recv, 2)
 
     arrived(g_recv, 1)
@@ -233,18 +235,11 @@
 
     lax.fori_loop(0, hid // 256, backward, 0)
 
-    def unproject(j, _):
-        value = dot(grad_pre[...], w_in[wide(j), :], ((1,), (1,)))
-        spread(2 * j, value[:, :LANES])
-        spread(2 * j + 1, value[:, LANES:])
-        return 0
-
-    lax.fori_loop(0, width // 256, unproject, 0)
-    to_blocks(b_send)
-    scatter(b_send, b_recv, 3)
+    side = math.isqrt(groups)
 
     def weight_terms(k, _):
-        to = (dp + k) % groups
+        turn = k * 5 % groups
+        to = (dp // side + turn // side) % side * side + (dp + turn) % side
         first_send[to] = dot(xs[:, lanes(to)], grad_pre[...], ((0,), (0,))).astype(BF16)
         second_send[to] = dot(hidden[...], gs[:, lanes(to)], ((0,), (0,))).astype(BF16)
         return to
@@ -267,6 +262,16 @@
     for which, source, target in ((4, first_send, first_recv), (5, second_send, second_recv)):
         pltpu.make_async_copy(source.at[dp], target.at[dp], own_sem.at[which]).start()
 
+    def unproject(j, _):
+        value = dot(grad_pre[...], w_in[wide(j), :], ((1,), (1,)))
+        spread(2 * j, value[:, :LANES])
+        spread(2 * j + 1, value[:, LANES:])
+        return 0
+
+    lax.fori_loop(0, width // 256, unproject, 0)
+    to_blocks(b_send)
+    scatter(b_send, b_recv, 3)
+
     arrived(o_recv, 2)
     from_blocks(o_recv)
     grad_gates_ref[...] = jnp.zeros_like(grad_gates_ref)
@@ -308,7 +313,6 @@
 
     lax.fori_loop(0, chunks, unmix, 0)
     sent(x_send, 0)
-    sent(g_send, 1)
     sent(o_send, 2)
     sent(b_send, 3)
     sent(first_send, 4)
@@ -326,7 +330,7 @@
     first = pltpu.VMEM((groups, width // groups, hid), BF16)
     second = pltpu.VMEM((groups, hid, width // groups), BF16)
     vmem = pl.BlockSpec(memory_space=pltpu.VMEM)
-    hbm = pl.BlockSpec(memory_space=pl.ANY)
+    hbm = pl.BlockSpec(memory_space=pltpu.HBM)
     mixed, grad_tokens, grad_gates, grad_first, grad_second = pl.pallas_call(
         functools.partial(kernel, groups, experts, capacity),
         out_shape=(

time: 349 us -> 313 us (0.90)
  the two profiles are of different devices: /device:TPU:605 before, /device:TPU:1 now
where the time goes in v2:
time: 313 us
  Pallas kernels  305 us (97%)
  local copies, waits for them, and re-layouts  7.26 us (2%)
    pallas_call x1, Pallas kernels, local(): pl.pallas_call(functools.partial(kernel, groups, experts, capacity), out_...  305 us
    unnamed x11, local copies, waits for them, and re-layouts  7.26 us

profile of v2, /device:TPU:1, one launch (start us, length us, event | category | flops | bytes accessed | tf_op | source)
XLA Modules:
  0.0 312.7 jit_solution(6959975119586631916)
XLA Ops:
  0.6 0.8 copy.11.routes_ref
  1.4 0.8 copy.12.gates_ref
  2.2 0.0 copy-start
  2.2 1.0 copy-done
  3.2 0.0 copy-start.1
  3.2 1.0 copy-done.1
  4.2 304.8 %shard_map.101 = (bf16[128,2048]{1,0:T(8,128)(2,1)S(1)}, bf16[128,2048]{1,0:T(8,128)(2,1)S(1)}, f32[128,1]{1,0:T(8,128)S(1)}, f32[128,768]{1,0:T(8,128)S(1)}, f32[768,128]{1,0:T(8,128)S(1)}) custom-call(bf16[128,2048]{1,0:T(8,128)(2,1)S(1)} %copy-done, bf16[128,2048]{1,0:T(8,128)(2,1)S(1)} %copy-done.1, bf16[2048,768]{1,0:T(8,128)(2,1)} %bitcast.6, ...), custom_call_target="tpu_custom_call" | custom-call | flops 3623878656 | bytes 18874368 | tf_op jit(solution)/shard_map/pallas_call | solution.py:334
  309.1 0.6 copy.13
  309.7 0.8 copy.18
  310.5 0.8 copy.19
  311.2 0.7 copy.20
  312.0 0.7 copy.21
Async XLA Ops:
  2.2 1.0 copy-start
  3.2 1.0 copy-start.1

commit v3 on v2

--- a/solution.py
+++ b/solution.py
@@ -28,9 +28,15 @@
     w_out_hbm,
     routes_ref,
     gates_ref,
+    mixed_hbm,
+    grad_tok_hbm,
+    grad_gates_hbm,
+    first_hbm,
+    second_hbm,
     mixed_ref,
     grad_tok_ref,
     grad_gates_ref,
+    gates_row,
     first_ref,
     second_ref,
     tok,
@@ -38,6 +44,8 @@
     w_in,
     w_out,
     select,
+    combine,
+    gates,
     stage,
     x_send,
     x_recv,
@@ -57,6 +65,7 @@
     second_send,
     second_recv,
     load_sem,
+    save_sem,
     own_sem,
     send_sem,
     recv_sem,
@@ -71,6 +80,18 @@
     block = capacity * chunks
     hid = hidden.shape[1]
 
+    saves = [
+        pltpu.make_async_copy(source, target, save_sem.at[i])
+        for i, (source, target) in enumerate(
+            (
+                (mixed_ref, mixed_hbm),
+                (gates_row, grad_gates_hbm),
+                (first_ref, first_hbm),
+                (second_ref, second_hbm),
+                (grad_tok_ref, grad_tok_hbm),
+            )
+        )
+    ]
     loads = [
         pltpu.make_async_copy(source, target, load_sem.at[i])
         for i, (source, target) in enumerate(
@@ -98,9 +119,12 @@
     lax.fori_loop(1, groups, greet_group, 0)
 
     def scatter(source, target, which):
-        pltpu.make_async_copy(source.at[me], target.at[me], own_sem.at[which]).start()
+        def fill(place):
+            part = stage[pl.ds(pl.multiple_of(place * block, block), block), :]
+            source[place] = part.astype(BF16)
 
         def send(place):
+            fill(place)
             pltpu.make_async_remote_copy(
                 src_ref=source.at[place],
                 dst_ref=target.at[me],
@@ -120,6 +144,8 @@
 
         lax.fori_loop(0, ring - 1, step, 0)
         send(z * 2 + 1 - core)
+        fill(me)
+        pltpu.make_async_copy(source.at[me], target.at[me], own_sem.at[which]).start()
 
     def arrived(target, which):
         others = target.at[pl.ds(0, target.shape[0] - 1)]
@@ -139,14 +165,6 @@
     def lanes(j):
         return pl.ds(pl.multiple_of(j * LANES, LANES), LANES)
 
-    def to_blocks(target):
-        def step(e, _):
-            part = stage[pl.ds(pl.multiple_of(e * block, block), block), :]
-            target[e] = part.astype(BF16)
-            return 0
-
-        lax.fori_loop(0, experts, step, 0, unroll=4)
-
     def from_blocks(source):
         def step(e, _):
             stage[pl.ds(pl.multiple_of(e * block, block), block), :] = source[e].astype(F32)
@@ -164,37 +182,39 @@
         lax.fori_loop(0, chunks, step, 0)
 
     route = routes_ref[...]
-    onehot = (route == lax.broadcasted_iota(jnp.int32, (rows, experts), 1)).astype(F32)
+    onehot = (route == lax.broadcasted_iota(jnp.int32, (experts, rows), 0)).astype(F32)
     before = (
         lax.broadcasted_iota(jnp.int32, (rows, rows), 0)
-        > lax.broadcasted_iota(jnp.int32, (rows, rows), 1)
+        < lax.broadcasted_iota(jnp.int32, (rows, rows), 1)
     ).astype(BF16)
-    earlier = dot(before, onehot.astype(BF16), ((1,), (0,)))
-    slot = jnp.sum(onehot * earlier, axis=1, keepdims=True).astype(jnp.int32)
+    earlier = dot(onehot.astype(BF16), before, ((1,), (0,)))
+    slot = jnp.sum(onehot * earlier, axis=0, keepdims=True).astype(jnp.int32)
     place = route * capacity + slot
-    select[...] = (place == lax.broadcasted_iota(jnp.int32, (rows, slots), 1)).astype(BF16)
+    chosen = (place == lax.broadcasted_iota(jnp.int32, (slots, rows), 0)).astype(F32)
+    select[...] = chosen.astype(BF16)
 
     loads[0].wait()
 
     def pick_tokens(j, _):
-        spread(j, dot(select[...], tok[:, lanes(j)], ((0,), (0,))))
+        spread(j, dot(select[...], tok[:, lanes(j)], ((1,), (0,))))
         return 0
 
     lax.fori_loop(0, chunks, pick_tokens, 0)
-    to_blocks(x_send)
     pl.semaphore_wait(barrier, experts - 1 + groups - 1)
     scatter(x_send, x_recv, 0)
 
+    gates[...] = jnp.transpose(jnp.broadcast_to(gates_ref[...], (rows, rows)))[:, :1]
     loads[1].wait()
 
     def pick_grads(j, _):
-        scaled = (gates_ref[...] * cot[:, lanes(j)].astype(F32)).astype(BF16)
-        spread(j, dot(select[...], scaled, ((0,), (0,))))
+        scaled = (gates[...] * cot[:, lanes(j)].astype(F32)).astype(BF16)
+        spread(j, dot(select[...], scaled, ((1,), (0,))))
         return 0
 
     lax.fori_loop(0, chunks, pick_grads, 0)
-    to_blocks(g_send)
     scatter(g_send, g_recv, 1)
+
+    combine[...] = jnp.transpose(chosen).astype(BF16)
 
     loads[2].wait()
     loads[3].wait()
@@ -219,7 +239,6 @@
         return 0
 
     lax.fori_loop(0, width // 256, project, 0)
-    to_blocks(o_send)
     sent(g_send, 1)
     scatter(o_send, o_recv, 2)
 
@@ -269,7 +288,6 @@
         return 0
 
     lax.fori_loop(0, width // 256, unproject, 0)
-    to_blocks(b_send)
     scatter(b_send, b_recv, 3)
 
     arrived(o_recv, 2)
@@ -277,14 +295,17 @@
     grad_gates_ref[...] = jnp.zeros_like(grad_gates_ref)
 
     def mix(j, _):
-        picked = dot(select[...], gathered(j).astype(BF16), ((1,), (0,)))
-        mixed_ref[:, lanes(j)] = (gates_ref[...] * picked).astype(BF16)
+        picked = dot(combine[...], gathered(j).astype(BF16), ((1,), (0,)))
+        mixed_ref[:, lanes(j)] = (gates[...] * picked).astype(BF16)
         grad_gates_ref[...] += jnp.sum(
             picked * cot[:, lanes(j)].astype(F32), axis=1, keepdims=True
         )
         return 0
 
     lax.fori_loop(0, chunks, mix, 0)
+    gates_row[...] = jnp.transpose(jnp.broadcast_to(grad_gates_ref[...], (rows, rows)))[:1, :]
+    saves[0].start()
+    saves[1].start()
 
     arrived(first_recv, 4)
     arrived(second_recv, 5)
@@ -302,21 +323,39 @@
 
     add_terms(first_ref, first_recv)
     add_terms(second_ref, second_recv)
+    saves[2].start()
+    saves[3].start()
 
     arrived(b_recv, 3)
     from_blocks(b_recv)
 
     def unmix(j, _):
-        picked = dot(select[...], gathered(j).astype(BF16), ((1,), (0,)))
+        picked = dot(combine[...], gathered(j).astype(BF16), ((1,), (0,)))
         grad_tok_ref[:, lanes(j)] = picked.astype(BF16)
         return 0
 
     lax.fori_loop(0, chunks, unmix, 0)
+    saves[4].start()
+    for save in saves:
+        save.wait()
     sent(x_send, 0)
     sent(o_send, 2)
     sent(b_send, 3)
     sent(first_send, 4)
     sent(second_send, 5)
+
+
+def hand_over(*refs):
+    sources, targets, held, come, gone = refs[:5], refs[5:10], refs[10:15], refs[15], refs[16]
+    loads = [pltpu.make_async_copy(sources[i], held[i], come.at[i]) for i in range(5)]
+    saves = [pltpu.make_async_copy(held[i], targets[i], gone.at[i]) for i in range(5)]
+    for load in loads:
+        load.start()
+    for load, save in zip(loads, saves):
+        load.wait()
+        save.start()
+    for save in saves:
+        save.wait()
 
 
 def local(tokens, routes, gates, w_in, w_out, out_grad):
@@ -330,24 +369,32 @@
     first = pltpu.VMEM((groups, width // groups, hid), BF16)
     second = pltpu.VMEM((groups, hid, width // groups), BF16)
     vmem = pl.BlockSpec(memory_space=pltpu.VMEM)
-    hbm = pl.BlockSpec(memory_space=pltpu.HBM)
-    mixed, grad_tokens, grad_gates, grad_first, grad_second = pl.pallas_call(
+    hbm = pl.BlockSpec(memory_space=pl.ANY)
+    results = pl.pallas_call(
         functools.partial(kernel, groups, experts, capacity),
         out_shape=(
             jax.ShapeDtypeStruct((rows, width), BF16),
             jax.ShapeDtypeStruct((rows, width), BF16),
-            jax.ShapeDtypeStruct((rows, 1), F32),
+            jax.ShapeDtypeStruct((1, rows), F32),
             jax.ShapeDtypeStruct((width // groups, hid), F32),
             jax.ShapeDtypeStruct((hid, width // groups), F32),
         ),
         in_specs=[hbm, hbm, hbm, hbm, vmem, vmem],
-        out_specs=[vmem] * 5,
+        out_specs=[hbm] * 5,
         scratch_shapes=[
+            pltpu.VMEM((rows, width), BF16),
+            pltpu.VMEM((rows, width), BF16),
+            pltpu.VMEM((rows, 1), F32),
+            pltpu.VMEM((1, rows), F32),
+            pltpu.VMEM((width // groups, hid), F32),
+            pltpu.VMEM((hid, width // groups), F32),
             pltpu.VMEM((rows, width), BF16),
             pltpu.VMEM((rows, width), BF16),
             pltpu.VMEM((width, hid), BF16),
             pltpu.VMEM((hid, width), BF16),
+            pltpu.VMEM((slots, rows), BF16),
             pltpu.VMEM((rows, slots), BF16),
+            pltpu.VMEM((rows, 1), F32),
             pltpu.VMEM((slots * chunks, LANES), F32),
             *([blocks] * 8),
             pltpu.VMEM((slots, width), BF16),
@@ -360,20 +407,39 @@
             second,
             second,
             pltpu.SemaphoreType.DMA((4,)),
+            pltpu.SemaphoreType.DMA((5,)),
             pltpu.SemaphoreType.DMA((6,)),
             pltpu.SemaphoreType.DMA((6,)),
             pltpu.SemaphoreType.DMA((6,)),
         ],
         compiler_params=pltpu.CompilerParams(
-            collective_id=0, has_side_effects=True, vmem_limit_bytes=50 * 2**20
+            collective_id=0, has_side_effects=True, vmem_limit_bytes=62 * 2**20
         ),
         cost_estimate=pl.CostEstimate(
             flops=12 * slots * width * hid,
             bytes_accessed=12 * width * hid,
             transcendentals=2 * slots * hid,
         ),
-    )(tokens, out_grad, w_in[0], w_out[0], routes, gates)
-    return (mixed, grad_tokens, grad_gates, grad_first[None], grad_second[None])
+    )(tokens, out_grad, w_in[0], w_out[0], routes.reshape(1, rows), gates.reshape(1, rows))
+    mixed, grad_tokens, grad_gates, grad_first, grad_second = pl.pallas_call(
+        hand_over,
+        out_shape=[jax.ShapeDtypeStruct(r.shape, r.dtype) for r in results],
+        in_specs=[hbm] * 5,
+        out_specs=[hbm] * 5,
+        scratch_shapes=[
+            *(pltpu.VMEM(r.shape, r.dtype) for r in results),
+            pltpu.SemaphoreType.DMA((5,)),
+            pltpu.SemaphoreType.DMA((5,)),
+        ],
+        compiler_params=pltpu.CompilerParams(vmem_limit_bytes=62 * 2**20),
+    )(*results)
+    return (
+        mixed,
+        grad_tokens,
+        grad_gates.reshape(rows, 1),
+        grad_first[None],
+        grad_second[None],
+    )
 
 
 def solution(mesh):

time: 313 us -> 309 us (0.987)
  local copies, waits for them, and re-layouts: 7.26 us -> 0 us
    unnamed x11 -> x0, local copies, waits for them, and re-layouts: 7.26 us -> none
where the time goes in v3:
time: 309 us
  Pallas kernels  308 us (100%)
    pallas_call x1, Pallas kernels, local(): pl.pallas_call(functools.partial(kernel, groups, experts, capacity), out_...  306 us

profile of v3, /device:TPU:1, one launch (start us, length us, event | category | flops | bytes accessed | tf_op | source)
XLA Modules:
  0.0 309.0 jit_solution(2204703490821110054)
XLA Ops:
  0.6 306.0 %shard_map.101 = (bf16[128,2048]{1,0:T(8,128)(2,1)}, bf16[128,2048]{1,0:T(8,128)(2,1)}, f32[1,128]{1,0:T(1,128)}, f32[128,768]{1,0:T(8,128)}, f32[768,128]{1,0:T(8,128)}) custom-call(bf16[128,2048]{1,0:T(8,128)(2,1)} %tok_hbm.1, bf16[128,2048]{1,0:T(8,128)(2,1)} %grad_hbm.1, bf16[2048,768]{1,0:T(8,128)(2,1)} %bitcast.7, bf16[768,2048]{1,0:T(8,128)(2,1)} %bitcast.8, ...), custom_call_target="tpu_custom_call" | custom-call | flops 3623878656 | bytes 18874368 | tf_op jit(solution)/shard_map/pallas_call | solution.py:373
  306.7 2.4 shard_map.102

commit v4 on v3

--- a/solution.py
+++ b/solution.py
@@ -135,7 +135,7 @@
             ).start()
 
         def step(i, _):
-            far = ring // 2 - (i + 1) // 2
+            far = i // 2 + 1 if which == 0 else ring // 2 - (i + 1) // 2
             sign = 1 - 2 * (i % 2)
             there = (z + sign * far + ring) % ring
             send(there * 2 + core)

time: 309 us -> 309 us (level)
  no operation moved by 1% of the time
where the time goes in v4:
time: 309 us
  Pallas kernels  308 us (100%)
    pallas_call x1, Pallas kernels, local(): pl.pallas_call(functools.partial(kernel, groups, experts, capacity), out_...  306 us

profile of v4, /device:TPU:1, one launch (start us, length us, event | category | flops | bytes accessed | tf_op | source)
XLA Modules:
  0.0 308.7 jit_solution(14547906741545629491)
XLA Ops:
  0.6 305.7 %shard_map.101 = (bf16[128,2048]{1,0:T(8,128)(2,1)}, bf16[128,2048]{1,0:T(8,128)(2,1)}, f32[1,128]{1,0:T(1,128)}, f32[128,768]{1,0:T(8,128)}, f32[768,128]{1,0:T(8,128)}) custom-call(bf16[128,2048]{1,0:T(8,128)(2,1)} %tok_hbm.1, bf16[128,2048]{1,0:T(8,128)(2,1)} %grad_hbm.1, bf16[2048,768]{1,0:T(8,128)(2,1)} %bitcast.7, bf16[768,2048]{1,0:T(8,128)(2,1)} %bitcast.8, ...), custom_call_target="tpu_custom_call" | custom-call | flops 3623878656 | bytes 18874368 | tf_op jit(solution)/shard_map/pallas_call | solution.py:373
  306.3 2.4 shard_map.102
